TPU v7x, 256 devices: a whole 4x4x8 slice. The times are simulated.
256 devices in a mesh: dp: 32 (over z_lo, x, core), rows: 8 (over z_hi, y).
Axes of the slice: x: 4, y: 4, z: 8 (z_hi: 2, z_lo: 4; z = z_hi * 4 + z_lo), core: 2. Of those that a mesh axis runs over, the one named last changes fastest.
Arguments:
- features: bfloat16 [64, 48, 64, 1024], P('dp', 'rows'), may hold values from -8 to 8
- first_atrous_weight: bfloat16 [3, 3, 1024, 256], P(None, None, 'dp'), may hold values from -0.0625 to 0.0625
- second_atrous_weight: bfloat16 [3, 3, 1024, 256], P(None, None, 'dp'), may hold values from -0.0625 to 0.0625
- third_atrous_weight: bfloat16 [3, 3, 1024, 256], P(None, None, 'dp'), may hold values from -0.0625 to 0.0625
- pointwise_weight: bfloat16 [1024, 256], replicated, may hold values from -0.1875 to 0.1875
- pooling_weight: bfloat16 [1024, 256], replicated, may hold values from -0.1875 to 0.1875
- projection_weight: bfloat16 [1280, 256], replicated, may hold values from -0.15625 to 0.15625
- branch_norm_gain: float32 [4, 256], replicated, may hold values from 0.25 to 1.75
- branch_norm_shift: float32 [4, 256], replicated, may hold values from -3 to 3
- projection_norm_gain: float32 [256], replicated, may hold values from 0.25 to 1.75
- projection_norm_shift: float32 [256], replicated, may hold values from -3 to 3
- ghost_group_index: int32 [64], replicated, may hold values from 0 to 15, as said below
Outputs:
- decoder_in: bfloat16 [64, 48, 64, 256], P(None, 'rows', 'dp')
Inputs may be any that keep to these rules, and one draw needn't show every extreme that they name: `ghost_group_index`: each of the 16 group ids names exactly 4 images.
All inputs are finite; a program needn't handle non-finite values.
Results may differ from a plain program's by a relative error of at most 0.0014.
The roundings to bfloat16 on the way count: a program that leaves them out, or rounds other values in their place, can miss the bound.
Values may be sent and summed in bfloat16 or wider, within the bound.
A program may use at most 128 MiB of HBM per device.

v0:
```python
import jax
import jax.numpy as jnp
from jax import lax
from jax.sharding import PartitionSpec as P

DILATION_FIRST = 12
DILATION_SECOND = 24
DILATION_THIRD = 36


def from_behind(array, axis, by):
    count = lax.axis_size(axis)
    pairs = [(i, i + by) for i in range(count) if 0 <= i + by < count]
    return lax.ppermute(array, axis, pairs)


def row_tap_list(block_tensor, kernel_row_slice, dilation_rate):
    partial_terms = jnp.einsum(
        "irwc,kco->irwko", block_tensor, kernel_row_slice, preferred_element_type=jnp.float32
    )
    map_width = block_tensor.shape[2]
    left_padding = jnp.pad(partial_terms[:, :, :, 0], ((0, 0), (0, 0), (dilation_rate, 0), (0, 0)))[
        :, :, :map_width
    ]
    right_padding = jnp.pad(
        partial_terms[:, :, :, 2], ((0, 0), (0, 0), (0, dilation_rate), (0, 0))
    )[:, :, dilation_rate:]
    return partial_terms[:, :, :, 1] + left_padding + right_padding


def dilated_result(features, kernel_weight, dilation_rate):
    step_offsets = dilation_rate // features.shape[1]
    running_sum = row_tap_list(features, kernel_weight[1], dilation_rate)
    for by_dev, tap_offset in ((step_offsets, 0), (-step_offsets, 2)):
        shifted_rows = from_behind(features, "rows", by_dev)
        running_sum = running_sum + row_tap_list(
            shifted_rows, kernel_weight[tap_offset], dilation_rate
        )
    return running_sum


def stats_terms(pre, onehot):
    first = jnp.sum(pre, axis=(1, 2))
    second = jnp.sum(pre * pre, axis=(1, 2))
    group_first = jnp.dot(onehot.T, first, precision=lax.Precision.HIGHEST)
    group_second = jnp.dot(onehot.T, second, precision=lax.Precision.HIGHEST)
    return (group_first, group_second)


def apply_norm(pre, onehot, total_first, total_second, count, gain, shift):
    mean = total_first / count
    var = total_second / count - mean * mean
    inv = lax.rsqrt(var + 1e-05)
    img_mean = jnp.dot(onehot, mean, precision=lax.Precision.HIGHEST)
    img_inv = jnp.dot(onehot, inv, precision=lax.Precision.HIGHEST)
    scaled = (pre - img_mean[:, None, None, :]) * img_inv[:, None, None, :] * gain + shift
    return jax.nn.relu(scaled).astype(jnp.bfloat16)


def project(joined, onehot, projection_weight, count, projection_norm_gain, projection_norm_shift):
    proj = jnp.einsum(
        "irwc,co->irwo", joined, projection_weight, preferred_element_type=jnp.float32
    )
    group_first, group_second = stats_terms(proj, onehot)
    total_first, total_second = lax.psum((group_first, group_second), ("dp", "rows"))
    return apply_norm(
        proj, onehot, total_first, total_second, count, projection_norm_gain, projection_norm_shift
    )


def shards(
    features,
    first_atrous_weight,
    second_atrous_weight,
    third_atrous_weight,
    pointwise_weight,
    pooling_weight,
    projection_weight,
    branch_norm_gain,
    branch_norm_shift,
    projection_norm_gain,
    projection_norm_shift,
    ghost_group_index,
):
    img_dev, rows_dev, cols, chans = features.shape
    dp_size = lax.axis_size("dp")
    rows_size = lax.axis_size("rows")
    images = img_dev * dp_size
    groups = images // 4
    pixels = rows_dev * rows_size * cols
    count = 4.0 * pixels
    start = lax.axis_index("dp") * img_dev
    labels = jnp.arange(groups, dtype=jnp.int32)
    all_hot = (ghost_group_index[:, None] == labels[None, :]).astype(jnp.float32)
    own_hot = lax.dynamic_slice_in_dim(all_hot, start, img_dev, 0)
    first_kernel, second_kernel, third_kernel = (
        lax.all_gather(first_atrous_weight, "dp", axis=2, tiled=True),
        lax.all_gather(second_atrous_weight, "dp", axis=2, tiled=True),
        lax.all_gather(third_atrous_weight, "dp", axis=2, tiled=True),
    )
    pointwise_output = jnp.einsum(
        "irwc,co->irwo", features, pointwise_weight, preferred_element_type=jnp.float32
    )
    pre = jnp.concatenate(
        [
            pointwise_output,
            dilated_result(features, first_kernel, DILATION_FIRST),
            dilated_result(features, second_kernel, DILATION_SECOND),
            dilated_result(features, third_kernel, DILATION_THIRD),
        ],
        -1,
    )
    group_first, group_second = stats_terms(pre, own_hot)
    pool_part = jnp.sum(features, axis=(1, 2), dtype=jnp.float32)
    pool_total = lax.psum(pool_part, "rows")
    total_first, total_second = lax.psum((group_first, group_second), ("dp", "rows"))
    branches = apply_norm(
        pre,
        own_hot,
        total_first,
        total_second,
        count,
        branch_norm_gain.reshape(-1),
        branch_norm_shift.reshape(-1),
    )
    pooled = (pool_total / pixels).astype(jnp.bfloat16)
    pool_act = jax.nn.relu(
        jnp.dot(pooled, pooling_weight, preferred_element_type=jnp.float32)
    ).astype(jnp.bfloat16)
    pool_map = jnp.broadcast_to(
        pool_act[:, None, None, :], (img_dev, rows_dev, cols, pool_act.shape[1])
    )
    joined = jnp.concatenate([branches, pool_map], -1)
    local_out = project(
        joined, own_hot, projection_weight, count, projection_norm_gain, projection_norm_shift
    )
    return lax.all_to_all(local_out, "dp", split_axis=2, concat_axis=0, tiled=True)


def solution(mesh):
    in_specs = (
        P("dp", "rows", None, None),
        P(None, None, "dp", None),
        P(None, None, "dp", None),
        P(None, None, "dp", None),
        P(),
        P(),
        P(),
        P(),
        P(),
        P(),
        P(),
        P(),
    )
    out_specs = P(None, "rows", "dp", None)
    return jax.shard_map(shards, mesh=mesh, in_specs=in_specs, out_specs=out_specs, check_vma=False)
```

profile of v0, /device:TPU:1, one launch (start us, length us, event | category | flops | bytes accessed | tf_op | source)
XLA Modules:
  0.0 726.8 jit_solution(7017526560821502395)
XLA Ops:
  6.5 0.7 all-gather.4.cloned.1.call-update
  7.3 0.7 all-gather.6.cloned.1.call-update
  8.1 0.7 all-gather.8.cloned.1.call-update
  8.8 1.3 collective-permute-start.1
  10.1 7.5 %collective-permute-start = (bf16[2,6,64,1024]{3,2,1,0:T(8,128)(2,1)}, bf16[2,6,64,1024]{3,2,1,0:T(8,128)(2,1)}, u32[]{:S(2)}, u32[]{:S(2)}) collective-permute-start(bf16[2,6,64,1024]{3,2,1,0:T(8,128)(2,1)} %param.12), channel_id=1, source_target_pairs={{0,2},{1,3},{2,4},{3,5},{4,6},{5,7},{8,10},{9,11},{10,12},{11,13},... | collective-permute-start | bytes 4718600 | tf_op jit(solution)/shard_map/ppermute | solution.py:14
  17.6 1.3 collective-permute-start.3
  18.9 11.2 %collective-permute-start.2 = (bf16[2,6,64,1024]{3,2,1,0:T(8,128)(2,1)}, bf16[2,6,64,1024]{3,2,1,0:T(8,128)(2,1)}, u32[]{:S(2)}, u32[]{:S(2)}) collective-permute-start(bf16[2,6,64,1024]{3,2,1,0:T(8,128)(2,1)} %param.12), channel_id=1, source_target_pairs={{0,4},{1,5},{2,6},{3,7},{8,12},{9,13},{10,14},{11,15},{16,20},{17,... | collective-permute-start | bytes 4718600 | tf_op jit(solution)/shard_map/ppermute | solution.py:14
  30.1 1.3 collective-permute-start.5
  31.4 0.7 dynamic-slice
  32.1 1.7 convert_reduce_fusion
  33.9 146.7 %psum.37 = f32[2,1024]{1,0:T(2,128)S(1)} all-reduce(f32[2,1024]{1,0:T(2,128)S(1)} %convert_reduce_fusion), channel_id=1, replica_groups=mesh['dp'=32,'rows'=8] {'rows'}, use_global_device_ids=true, to_apply=%region_5.6 | all-reduce | flops 2048 | bytes 16384 | tf_op jit(solution)/shard_map/psum | solution.py:115
  180.5 2.1 fusion.49
  182.7 2.4 collective-permute-start.4
  185.1 3.4 fusion.10
  188.5 1.4 slice_bitcast_fusion.36
  189.9 2.8 fusion.11
  192.7 1.4 slice_bitcast_fusion.39
  194.1 1.4 fusion.12
  195.5 1.3 slice_bitcast_fusion.42
  196.8 0.6 copy-done.17
  197.4 90.0 %all-gather.6.cloned.1.call-done = bf16[3,3,1024,256]{3,2,1,0:T(8,128)(2,1)} async-done(((bf16[3,3,32,256]{3,2,1,0:T(8,128)(2,1)}), bf16[3,3,1024,256]{3,2,1,0:T(8,128)(2,1)}) %all-gather.6.cloned.1.call-update) | async-done | bytes 4718608 | tf_op jit(solution)/shard_map/all_gather | solution.py:98
  287.4 3.4 fusion.7
  290.8 1.4 slice_bitcast_fusion.27
  292.3 2.8 fusion.8
  295.1 1.4 slice_bitcast_fusion.30
  296.5 1.4 fusion.9
  297.9 1.5 slice_bitcast_fusion.33
  299.3 0.5 copy-done.20
  299.8 61.1 %all-gather.8.cloned.1.call-done = bf16[3,3,1024,256]{3,2,1,0:T(8,128)(2,1)} async-done(((bf16[3,3,32,256]{3,2,1,0:T(8,128)(2,1)}), bf16[3,3,1024,256]{3,2,1,0:T(8,128)(2,1)}) %all-gather.8.cloned.1.call-update) | async-done | bytes 4718608 | tf_op jit(solution)/shard_map/all_gather | solution.py:99
  361.0 3.4 fusion.4
  364.5 2.8 fusion.5
  367.3 0.1 slice_bitcast_fusion.21
  367.5 1.4 fusion.6
  369.1 0.9 copy-done.3
  370.0 0.2 copy-done.4
  370.3 0.2 copy-done.5
  370.5 0.2 copy-done.6
  370.8 2.3 fusion.26
  373.1 0.2 copy-done.12
  373.3 0.2 copy-done.13
  373.5 0.2 copy-done.14
  373.8 1.9 fusion.34
  375.7 0.6 fusion.42
  376.3 0.9 copy-done.1
  377.2 0.4 fusion.48
  377.6 0.9 fusion.79
  378.5 0.9 fusion.78
  379.5 0.2 fusion.22
  379.6 0.7 copy.119
  380.3 0.7 copy.120
  381.0 237.9 %all-reduce.22.cloned.1.call-done = (f32[16,1024]{1,0:T(8,128)}, f32[16,1024]{1,0:T(8,128)}) async-done(((f32[16,1024]{1,0:T(8,128)}, f32[16,1024]{1,0:T(8,128)}), (f32[16,1024]{1,0:T(8,128)}, f32[16,1024]{1,0:T(8,128)})) %all-reduce.22.cloned.1.call-update) | async-done | bytes 131088 | tf_op jit(solution)/shard_map/psum | solution.py:116
  618.9 1.0 fusion.58
  620.0 1.1 fusion.51
  621.0 1.7 maximum_convert_fusion
  622.8 0.7 fusion.96
  623.6 0.3 fusion.77
  623.8 0.3 fusion.76
  624.1 76.6 %all-reduce.18 = (f32[16,256]{1,0:T(8,128)S(1)}, f32[16,256]{1,0:T(8,128)S(1)}) all-reduce(f32[16,256]{1,0:T(8,128)S(1)} %fusion.76, f32[16,256]{1,0:T(8,128)S(1)} %fusion.77), channel_id=1, replica_groups=mesh['dp'=32,'rows'=8] {'dp','rows'}, use_global_device_ids=true, to_apply=%region_9.10 | all-reduce | flops 8192 | bytes 65536 | tf_op jit(solution)/shard_map/psum | solution.py:65
  700.7 0.2 fusion.70
  700.9 0.2 fusion.63
  701.1 0.2 maximum_convert_fusion.1
  701.2 0.4 copy.97
  701.6 17.6 %all_to_all.18 = bf16[2,6,64,256]{3,0,1,2:T(2,128)(2,1)S(1)} all-to-all(bf16[2,6,64,256]{3,0,1,2:T(2,128)(2,1)S(1)} %copy.97), channel_id=1, replica_groups=mesh['dp'=32,'rows'=8] {'dp'}, dimensions={2} | all-to-all | bytes 786432 | tf_op jit(solution)/shard_map/all_to_all | solution.py:137
  719.3 1.0 copy.98
  (59 shorter events, 0.6 us)
Async XLA Ops:
  6.5 616.3 %copy-start = (bf16[1280,256]{1,0:T(8,128)(2,1)S(1)}, bf16[1280,256]{1,0:T(8,128)(2,1)}, u32[]{:S(2)}) copy-start(bf16[1280,256]{1,0:T(8,128)(2,1)} %param.18) | copy-start | bytes 1966084
  6.5 178.6 %all-gather.4.cloned.1.call-start = ((), (), s32[]{:S(2)}) async-start(), calls=%async_computation.1 | async-start | bytes 4866048 | tf_op jit(solution)/shard_map/all_gather | solution.py:97
  7.3 280.2 %all-gather.6.cloned.1.call-start = ((), (), s32[]{:S(2)}) async-start(), calls=%async_computation.2 | async-start | bytes 4866048 | tf_op jit(solution)/shard_map/all_gather | solution.py:98
  8.0 174.6 %copy-start.2 = (bf16[2,6,64,1024]{3,2,1,0:T(8,128)(2,1)S(1)}, bf16[2,6,64,1024]{3,2,1,0:T(8,128)(2,1)}, u32[]{:S(2)}) copy-start(bf16[2,6,64,1024]{3,2,1,0:T(8,128)(2,1)} %param.12) | copy-start | bytes 4718596
  8.0 352.9 %all-gather.8.cloned.1.call-start = ((), (), s32[]{:S(2)}) async-start(), calls=%async_computation.3 | async-start | bytes 4866048 | tf_op jit(solution)/shard_map/all_gather | solution.py:99
  8.8 610.2 %all-reduce.22.cloned.1.call-start = ((), (), s32[]{:S(2)}) async-start(), calls=%async_computation.4 | async-start | bytes 262144 | tf_op jit(solution)/shard_map/psum | solution.py:116
  8.8 173.8 %collective-permute-start.1 = (bf16[2,6,64,1024]{3,2,1,0:T(8,128)(2,1)}, bf16[2,6,64,1024]{3,2,1,0:T(8,128)(2,1)}, u32[]{:S(2)}, u32[]{:S(2)}) collective-permute-start(bf16[2,6,64,1024]{3,2,1,0:T(8,128)(2,1)} %param.12), channel_id=1, source_target_pairs={{2,0},{3,1},{4,2},{5,3},{6,4},{7,5},{10,8},{11,9},{12,10},{13,11},... | collective-permute-start | bytes 4718600 | tf_op jit(solution)/shard_map/ppermute | solution.py:14
  10.1 179.8 %collective-permute-start = (bf16[2,6,64,1024]{3,2,1,0:T(8,128)(2,1)}, bf16[2,6,64,1024]{3,2,1,0:T(8,128)(2,1)}, u32[]{:S(2)}, u32[]{:S(2)}) collective-permute-start(bf16[2,6,64,1024]{3,2,1,0:T(8,128)(2,1)} %param.12), channel_id=1, source_target_pairs={{0,2},{1,3},{2,4},{3,5},{4,6},{5,7},{8,10},{9,11},{10,12},{11,13},... | collective-permute-start | bytes 4718600 | tf_op jit(solution)/shard_map/ppermute | solution.py:14
  17.6 179.9 %collective-permute-start.3 = (bf16[2,6,64,1024]{3,2,1,0:T(8,128)(2,1)}, bf16[2,6,64,1024]{3,2,1,0:T(8,128)(2,1)}, u32[]{:S(2)}, u32[]{:S(2)}) collective-permute-start(bf16[2,6,64,1024]{3,2,1,0:T(8,128)(2,1)} %param.12), channel_id=1, source_target_pairs={{4,0},{5,1},{6,2},{7,3},{12,8},{13,9},{14,10},{15,11},{20,16},{21,... | collective-permute-start | bytes 4718600 | tf_op jit(solution)/shard_map/ppermute | solution.py:14
  18.9 273.4 %collective-permute-start.2 = (bf16[2,6,64,1024]{3,2,1,0:T(8,128)(2,1)}, bf16[2,6,64,1024]{3,2,1,0:T(8,128)(2,1)}, u32[]{:S(2)}, u32[]{:S(2)}) collective-permute-start(bf16[2,6,64,1024]{3,2,1,0:T(8,128)(2,1)} %param.12), channel_id=1, source_target_pairs={{0,4},{1,5},{2,6},{3,7},{8,12},{9,13},{10,14},{11,15},{16,20},{17,... | collective-permute-start | bytes 4718600 | tf_op jit(solution)/shard_map/ppermute | solution.py:14
  30.1 269.7 %collective-permute-start.5 = (bf16[2,6,64,1024]{3,2,1,0:T(8,128)(2,1)}, bf16[2,6,64,1024]{3,2,1,0:T(8,128)(2,1)}, u32[]{:S(2)}, u32[]{:S(2)}) collective-permute-start(bf16[2,6,64,1024]{3,2,1,0:T(8,128)(2,1)} %param.12), channel_id=1, source_target_pairs={{6,0},{7,1},{14,8},{15,9},{22,16},{23,17},{30,24},{31,25},{38,32},... | collective-permute-start | bytes 4718600 | tf_op jit(solution)/shard_map/ppermute | solution.py:14
  182.7 181.9 %collective-permute-start.4 = (bf16[2,6,64,1024]{3,2,1,0:T(8,128)(2,1)S(1)}, bf16[2,6,64,1024]{3,2,1,0:T(8,128)(2,1)}, u32[]{:S(2)}, u32[]{:S(2)}) collective-permute-start(bf16[2,6,64,1024]{3,2,1,0:T(8,128)(2,1)S(1)} %copy-done.2), channel_id=1, source_target_pairs={{0,6},{1,7},{8,14},{9,15},{16,22},{17,23},{24,30},{25,31},{32,38},... | collective-permute-start | bytes 4718600 | tf_op jit(solution)/shard_map/ppermute | solution.py:14
  185.1 4.8 copy-start.26
  188.5 4.2 copy-start.15
  192.7 2.8 copy-start.16
  195.5 2.0 copy-start.17
  287.4 4.8 copy-start.25
  290.8 4.2 copy-start.18
  295.1 2.8 copy-start.19
  297.9 2.0 copy-start.20
  361.0 3.6 copy-start.24
  367.5 1.6 copy-start.7
  367.5 1.6 copy-start.8
  368.9 1.1 copy-start.3
  368.9 1.4 copy-start.4
  368.9 1.6 copy-start.5
  368.9 1.8 copy-start.6
  370.8 2.3 copy-start.9
  370.8 2.3 copy-start.10
  370.8 2.3 copy-start.11
  370.8 2.5 copy-start.12
  370.8 2.8 copy-start.13
  370.8 3.0 copy-start.14
  376.3 0.9 copy-start.1
  377.2 2.2 copy-start.21
  622.8 78.2 %copy-start.22 = (f32[256]{0:T(256)S(1)}, f32[256]{0:T(256)}, u32[]{:S(2)}) copy-start(f32[256]{0:T(256)} %param.22) | copy-start | bytes 3076
  622.8 78.2 %copy-start.23 = (f32[256]{0:T(256)S(1)}, f32[256]{0:T(256)}, u32[]{:S(2)}) copy-start(f32[256]{0:T(256)} %param.21) | copy-start | bytes 3076
Sparse Core Ops, SparseCore 0:
  9.2 144.8 all-gather.3
  156.0 131.4 all-gather.5
  289.3 71.6 all-gather.7
  379.6 239.3 all-reduce.21
where the time goes:
time: 728 us; the launch traced here: 727 us
  waiting for transfers between devices  391 us (54%)
  blocking collectives  241 us (33%)
  matrix products  30.6 us (4%)
  starting transfers between devices  25.1 us (3%)
  local copies, waits for them, and re-layouts  16.8 us (2%)
  between operations  13.6 us (2%)
  other arithmetic  8.76 us (1%)
    psum x1, waiting for transfers between devices, shards(): lax.psum((group_first, group_second), ('dp', 'rows'))  238 us
    psum x1, blocking collectives, shards(): pool_total = lax.psum(pool_part, 'rows')  147 us
    all_gather x1, waiting for transfers between devices, shards(): lax.all_gather(second_atrous_weight, 'dp', axis=2, tiled=True)  90 us
    psum x1, blocking collectives, project(): lax.psum((group_first, group_second), ('dp', 'rows'))  76.6 us
    all_gather x1, waiting for transfers between devices, shards(): lax.all_gather(third_atrous_weight, 'dp', axis=2, tiled=True)  61.1 us
    ppermute x6, starting transfers between devices, from_behind(): return lax.ppermute(array, axis, pairs)  25 us
    dot_general x9, matrix products, row_tap_list(): jnp.einsum('irwc,kco->irwko', block_tensor, kernel_row_slice, preferred_e...  22.8 us
    all_to_all x1, blocking collectives, shards(): lax.all_to_all(local_out, 'dp', split_axis=2, concat_axis=0, tiled=True)  17.6 us
  transfers between devices with their start and end apart: 10, of which 3 were waited for; matrix products, arithmetic and copies ran while one was open for 5% of the time, Pallas kernels for 0%

commit v1 on v0

--- a/solution.py
+++ b/solution.py
@@ -62,7 +62,7 @@
         "irwc,co->irwo", joined, projection_weight, preferred_element_type=jnp.float32
     )
     group_first, group_second = stats_terms(proj, onehot)
-    total_first, total_second = lax.psum((group_first, group_second), ("dp", "rows"))
+    total_first, total_second = lax.psum(lax.psum((group_first, group_second), "rows"), "dp")
     return apply_norm(
         proj, onehot, total_first, total_second, count, projection_norm_gain, projection_norm_shift
     )

time: 728 us -> 836 us (1.15)
  blocking collectives: 241 us -> 349 us
    psum x1 -> x2, blocking collectives: 76.6 us -> 179 us  [the longest x1 135 us: project(): lax.psum(lax.psum((group_first, group_second), 'rows'), 'dp')]
  transfers between devices with their start and end apart: 10 -> 10, of which waited for: 3 -> 3; matrix products, arithmetic and copies ran while one was open for 5% -> 4% of each run, Pallas kernels for 0% -> 0%
where the time goes in v1:
time: 836 us
  waiting for transfers between devices  392 us (47%)
  blocking collectives  349 us (42%)
  matrix products  30.6 us (4%)
  starting transfers between devices  25.1 us (3%)
  local copies, waits for them, and re-layouts  16.8 us (2%)
  between operations  13.6 us (2%)
  other arithmetic  8.76 us (1%)
    psum x1, waiting for transfers between devices, shards(): lax.psum((group_first, group_second), ('dp', 'rows'))  238 us
    psum x1, blocking collectives, shards(): pool_total = lax.psum(pool_part, 'rows')  147 us
    psum x1, blocking collectives, project(): lax.psum(lax.psum((group_first, group_second), 'rows'), 'dp')  135 us
    all_gather x1, waiting for transfers between devices, shards(): lax.all_gather(second_atrous_weight, 'dp', axis=2, tiled=True)  88.2 us
    all_gather x1, waiting for transfers between devices, shards(): lax.all_gather(third_atrous_weight, 'dp', axis=2, tiled=True)  63.8 us
    psum x1, blocking collectives, project(): lax.psum((group_first, group_second), 'rows')  44.1 us
    ppermute x6, starting transfers between devices, from_behind(): return lax.ppermute(array, axis, pairs)  25 us
    all_to_all x1, blocking collectives, shards(): lax.all_to_all(local_out, 'dp', split_axis=2, concat_axis=0, tiled=True)  22.8 us
  transfers between devices with their start and end apart: 10, of which 3 were waited for; matrix products, arithmetic and copies ran while one was open for 4% of the time, Pallas kernels for 0%

profile of v1, /device:TPU:1, one launch (start us, length us, event | category | flops | bytes accessed | tf_op | source)
XLA Modules:
  0.0 835.5 jit_solution(3345358283914562463)
XLA Ops:
  6.5 0.7 all-gather.4.cloned.1.call-update
  7.3 0.7 all-gather.6.cloned.1.call-update
  8.1 0.7 all-gather.8.cloned.1.call-update
  8.8 1.3 collective-permute-start.1
  10.1 7.5 collective-permute-start
  17.6 1.3 collective-permute-start.3
  18.9 11.3 %collective-permute-start.2 = (bf16[2,6,64,1024]{3,2,1,0:T(8,128)(2,1)}, bf16[2,6,64,1024]{3,2,1,0:T(8,128)(2,1)}, u32[]{:S(2)}, u32[]{:S(2)}) collective-permute-start(bf16[2,6,64,1024]{3,2,1,0:T(8,128)(2,1)} %param.12), channel_id=1, source_target_pairs={{0,4},{1,5},{2,6},{3,7},{8,12},{9,13},{10,14},{11,15},{16,20},{17,... | collective-permute-start | bytes 4718600 | tf_op jit(solution)/shard_map/ppermute | solution.py:14
  30.1 1.3 collective-permute-start.5
  31.4 0.7 dynamic-slice
  32.2 1.7 convert_reduce_fusion
  33.9 146.6 %psum.51 = f32[2,1024]{1,0:T(2,128)S(1)} all-reduce(f32[2,1024]{1,0:T(2,128)S(1)} %convert_reduce_fusion), channel_id=1, replica_groups=mesh['dp'=32,'rows'=8] {'rows'}, use_global_device_ids=true, to_apply=%region_5.6 | all-reduce | flops 2048 | bytes 16384 | tf_op jit(solution)/shard_map/psum | solution.py:115
  180.5 2.1 fusion.49
  182.7 2.4 collective-permute-start.4
  185.1 3.4 fusion.10
  188.5 1.4 slice_bitcast_fusion.36
  189.9 2.8 fusion.11
  192.7 1.4 slice_bitcast_fusion.39
  194.1 1.4 fusion.12
  195.5 1.4 slice_bitcast_fusion.42
  196.9 0.6 copy-done.17
  197.5 88.2 %all-gather.6.cloned.1.call-done = bf16[3,3,1024,256]{3,2,1,0:T(8,128)(2,1)} async-done(((bf16[3,3,32,256]{3,2,1,0:T(8,128)(2,1)}), bf16[3,3,1024,256]{3,2,1,0:T(8,128)(2,1)}) %all-gather.6.cloned.1.call-update) | async-done | bytes 4718608 | tf_op jit(solution)/shard_map/all_gather | solution.py:98
  285.6 3.4 fusion.7
  289.1 1.4 slice_bitcast_fusion.27
  290.5 2.8 fusion.8
  293.3 1.4 slice_bitcast_fusion.30
  294.7 1.4 fusion.9
  296.1 1.4 slice_bitcast_fusion.33
  297.6 0.5 copy-done.20
  298.1 63.8 %all-gather.8.cloned.1.call-done = bf16[3,3,1024,256]{3,2,1,0:T(8,128)(2,1)} async-done(((bf16[3,3,32,256]{3,2,1,0:T(8,128)(2,1)}), bf16[3,3,1024,256]{3,2,1,0:T(8,128)(2,1)}) %all-gather.8.cloned.1.call-update) | async-done | bytes 4718608 | tf_op jit(solution)/shard_map/all_gather | solution.py:99
  361.9 3.4 fusion.4
  365.5 2.8 fusion.5
  368.4 1.4 fusion.6
  370.0 0.9 copy-done.3
  371.0 0.2 copy-done.4
  371.2 0.2 copy-done.5
  371.4 0.2 copy-done.6
  371.7 2.3 fusion.26
  374.0 0.2 copy-done.12
  374.2 0.2 copy-done.13
  374.5 0.2 copy-done.14
  374.7 1.9 fusion.34
  376.6 0.6 fusion.42
  377.2 0.9 copy-done.1
  378.1 0.4 fusion.48
  378.5 0.9 fusion.79
  379.4 0.9 fusion.78
  380.4 0.2 fusion.22
  380.6 0.7 copy.119
  381.3 0.7 copy.120
  382.0 237.9 %all-reduce.23.cloned.1.call-done = (f32[16,1024]{1,0:T(8,128)}, f32[16,1024]{1,0:T(8,128)}) async-done(((f32[16,1024]{1,0:T(8,128)}, f32[16,1024]{1,0:T(8,128)}), (f32[16,1024]{1,0:T(8,128)}, f32[16,1024]{1,0:T(8,128)})) %all-reduce.23.cloned.1.call-update) | async-done | bytes 131088 | tf_op jit(solution)/shard_map/psum | solution.py:116
  619.9 1.0 fusion.58
  620.9 1.1 fusion.51
  622.0 1.7 maximum_convert_fusion
  623.8 0.7 fusion.96
  624.5 0.3 fusion.77
  624.7 0.3 fusion.76
  625.0 44.1 %all-reduce.20 = (f32[16,256]{1,0:T(8,128)S(1)}, f32[16,256]{1,0:T(8,128)S(1)}) all-reduce(f32[16,256]{1,0:T(8,128)S(1)} %fusion.76, f32[16,256]{1,0:T(8,128)S(1)} %fusion.77), channel_id=1, replica_groups=mesh['dp'=32,'rows'=8] {'rows'}, use_global_device_ids=true, to_apply=%region_10.11 | all-reduce | flops 8192 | bytes 65536 | tf_op jit(solution)/shard_map/psum | solution.py:65
  669.1 135.1 %all-reduce.19 = (f32[16,256]{1,0:T(8,128)S(1)}, f32[16,256]{1,0:T(8,128)S(1)}) all-reduce(f32[16,256]{1,0:T(8,128)S(1)} %get-tuple-element.13, f32[16,256]{1,0:T(8,128)S(1)} %get-tuple-element.14), channel_id=1, replica_groups=mesh['dp'=32,'rows'=8] {'dp'}, use_global_device_ids=true, to_apply=%region_11.12 | all-reduce | flops 8192 | bytes 65536 | tf_op jit(solution)/shard_map/psum | solution.py:65
  804.2 0.2 fusion.70
  804.4 0.2 fusion.63
  804.6 0.2 maximum_convert_fusion.1
  804.8 0.4 copy.97
  805.2 22.8 %all_to_all.18 = bf16[2,6,64,256]{3,0,1,2:T(2,128)(2,1)S(1)} all-to-all(bf16[2,6,64,256]{3,0,1,2:T(2,128)(2,1)S(1)} %copy.97), channel_id=1, replica_groups=mesh['dp'=32,'rows'=8] {'dp'}, dimensions={2} | all-to-all | bytes 786432 | tf_op jit(solution)/shard_map/all_to_all | solution.py:137
  828.0 1.0 copy.98
  (60 shorter events, 0.7 us)
Async XLA Ops:
  6.5 617.2 %copy-start = (bf16[1280,256]{1,0:T(8,128)(2,1)S(1)}, bf16[1280,256]{1,0:T(8,128)(2,1)}, u32[]{:S(2)}) copy-start(bf16[1280,256]{1,0:T(8,128)(2,1)} %param.18) | copy-start | bytes 1966084
  6.5 178.6 %all-gather.4.cloned.1.call-start = ((), (), s32[]{:S(2)}) async-start(), calls=%async_computation.1 | async-start | bytes 4866048 | tf_op jit(solution)/shard_map/all_gather | solution.py:97
  7.3 278.4 %all-gather.6.cloned.1.call-start = ((), (), s32[]{:S(2)}) async-start(), calls=%async_computation.2 | async-start | bytes 4866048 | tf_op jit(solution)/shard_map/all_gather | solution.py:98
  8.0 174.6 %copy-start.2 = (bf16[2,6,64,1024]{3,2,1,0:T(8,128)(2,1)S(1)}, bf16[2,6,64,1024]{3,2,1,0:T(8,128)(2,1)}, u32[]{:S(2)}) copy-start(bf16[2,6,64,1024]{3,2,1,0:T(8,128)(2,1)} %param.12) | copy-start | bytes 4718596
  8.0 353.8 %all-gather.8.cloned.1.call-start = ((), (), s32[]{:S(2)}) async-start(), calls=%async_computation.3 | async-start | bytes 4866048 | tf_op jit(solution)/shard_map/all_gather | solution.py:99
  8.8 611.1 %all-reduce.23.cloned.1.call-start = ((), (), s32[]{:S(2)}) async-start(), calls=%async_computation.4 | async-start | bytes 262144 | tf_op jit(solution)/shard_map/psum | solution.py:116
  8.8 173.8 %collective-permute-start.1 = (bf16[2,6,64,1024]{3,2,1,0:T(8,128)(2,1)}, bf16[2,6,64,1024]{3,2,1,0:T(8,128)(2,1)}, u32[]{:S(2)}, u32[]{:S(2)}) collective-permute-start(bf16[2,6,64,1024]{3,2,1,0:T(8,128)(2,1)} %param.12), channel_id=1, source_target_pairs={{2,0},{3,1},{4,2},{5,3},{6,4},{7,5},{10,8},{11,9},{12,10},{13,11},... | collective-permute-start | bytes 4718600 | tf_op jit(solution)/shard_map/ppermute | solution.py:14
  10.1 179.8 %collective-permute-start = (bf16[2,6,64,1024]{3,2,1,0:T(8,128)(2,1)}, bf16[2,6,64,1024]{3,2,1,0:T(8,128)(2,1)}, u32[]{:S(2)}, u32[]{:S(2)}) collective-permute-start(bf16[2,6,64,1024]{3,2,1,0:T(8,128)(2,1)} %param.12), channel_id=1, source_target_pairs={{0,2},{1,3},{2,4},{3,5},{4,6},{5,7},{8,10},{9,11},{10,12},{11,13},... | collective-permute-start | bytes 4718600 | tf_op jit(solution)/shard_map/ppermute | solution.py:14
  17.6 179.9 %collective-permute-start.3 = (bf16[2,6,64,1024]{3,2,1,0:T(8,128)(2,1)}, bf16[2,6,64,1024]{3,2,1,0:T(8,128)(2,1)}, u32[]{:S(2)}, u32[]{:S(2)}) collective-permute-start(bf16[2,6,64,1024]{3,2,1,0:T(8,128)(2,1)} %param.12), channel_id=1, source_target_pairs={{4,0},{5,1},{6,2},{7,3},{12,8},{13,9},{14,10},{15,11},{20,16},{21,... | collective-permute-start | bytes 4718600 | tf_op jit(solution)/shard_map/ppermute | solution.py:14
  18.9 271.6 %collective-permute-start.2 = (bf16[2,6,64,1024]{3,2,1,0:T(8,128)(2,1)}, bf16[2,6,64,1024]{3,2,1,0:T(8,128)(2,1)}, u32[]{:S(2)}, u32[]{:S(2)}) collective-permute-start(bf16[2,6,64,1024]{3,2,1,0:T(8,128)(2,1)} %param.12), channel_id=1, source_target_pairs={{0,4},{1,5},{2,6},{3,7},{8,12},{9,13},{10,14},{11,15},{16,20},{17,... | collective-permute-start | bytes 4718600 | tf_op jit(solution)/shard_map/ppermute | solution.py:14
  30.1 267.9 %collective-permute-start.5 = (bf16[2,6,64,1024]{3,2,1,0:T(8,128)(2,1)}, bf16[2,6,64,1024]{3,2,1,0:T(8,128)(2,1)}, u32[]{:S(2)}, u32[]{:S(2)}) collective-permute-start(bf16[2,6,64,1024]{3,2,1,0:T(8,128)(2,1)} %param.12), channel_id=1, source_target_pairs={{6,0},{7,1},{14,8},{15,9},{22,16},{23,17},{30,24},{31,25},{38,32},... | collective-permute-start | bytes 4718600 | tf_op jit(solution)/shard_map/ppermute | solution.py:14
  182.7 182.8 %collective-permute-start.4 = (bf16[2,6,64,1024]{3,2,1,0:T(8,128)(2,1)S(1)}, bf16[2,6,64,1024]{3,2,1,0:T(8,128)(2,1)}, u32[]{:S(2)}, u32[]{:S(2)}) collective-permute-start(bf16[2,6,64,1024]{3,2,1,0:T(8,128)(2,1)S(1)} %copy-done.2), channel_id=1, source_target_pairs={{0,6},{1,7},{8,14},{9,15},{16,22},{17,23},{24,30},{25,31},{32,38},... | collective-permute-start | bytes 4718600 | tf_op jit(solution)/shard_map/ppermute | solution.py:14
  185.1 4.8 copy-start.26
  188.5 4.2 copy-start.15
  192.7 2.8 copy-start.16
  195.5 2.0 copy-start.17
  285.6 4.9 copy-start.25
  289.1 4.2 copy-start.18
  293.3 2.8 copy-start.19
  296.1 1.9 copy-start.20
  361.9 3.6 copy-start.24
  368.4 1.6 copy-start.7
  368.4 1.6 copy-start.8
  369.8 1.1 copy-start.3
  369.8 1.4 copy-start.4
  369.8 1.6 copy-start.5
  369.9 1.8 copy-start.6
  371.7 2.3 copy-start.9
  371.7 2.3 copy-start.10
  371.7 2.3 copy-start.11
  371.7 2.5 copy-start.12
  371.7 2.8 copy-start.13
  371.7 3.0 copy-start.14
  377.2 0.9 copy-start.1
  378.1 2.2 copy-start.21
  623.8 180.8 %copy-start.22 = (f32[256]{0:T(256)S(1)}, f32[256]{0:T(256)}, u32[]{:S(2)}) copy-start(f32[256]{0:T(256)} %param.22) | copy-start | bytes 3076
  623.8 180.8 %copy-start.23 = (f32[256]{0:T(256)S(1)}, f32[256]{0:T(256)}, u32[]{:S(2)}) copy-start(f32[256]{0:T(256)} %param.21) | copy-start | bytes 3076
Sparse Core Ops, SparseCore 0:
  9.2 141.1 all-gather.3
  152.3 133.2 all-gather.5
  287.5 74.2 all-gather.7
  380.5 239.3 all-reduce.22
